TPU v7x, 32 devices: a whole 2x2x4 slice. The times are simulated.
32 devices in a mesh: layer: 2 (over x), example: 16 (over z, y, core).
Axes of the slice: x: 2, y: 2, z: 4, core: 2. Of those that a mesh axis runs over, the one named last changes fastest.
Arguments:
- adapter_input: bfloat16 [2, 8, 65536], P('layer', None, 'example'), may hold values from -4 to 4
- output_gradient: bfloat16 [2, 65536, 512], P('layer', 'example'), may hold values from -4 to 4
- projection: bfloat16 [2, 4, 512, 128], P('layer'), may hold values from -0.25 to 0.25
- input_block_index: int32 [2, 4, 4], P('layer'), may hold values from 0 to 31
- turn_token_length: int32 [2048], P('example'), may hold values from 1 to 32, as said below
- turn_to_example: int32 [2048], P('example'), may hold values from 0 to 1023, as said below
Outputs:
- factor: float32 [512, 512], P('example')
- whitened: float32 [1024, 512], P(('example', 'layer'))
Inputs may be any that keep to these rules, and one draw needn't show every extreme that they name: `turn_token_length`: within each shard of 128 turns the lengths add up to at most 4096. `turn_to_example`: the turns of shard s carry the example numbers s * 64 to (s + 1) * 64 - 1, never falling, each at least once.
All inputs are finite; a program needn't handle non-finite values.
Results may differ from a plain program's by a relative error of at most 0.0033.
Values sent between devices are 32-bit elements; how exact they have to be, the bound alone decides.
A program may use at most 64 MiB of HBM per device.

v0:
```python
import math

import jax
import jax.numpy as jnp
from jax import lax
from jax.sharding import PartitionSpec as P

EX_DEV = 64


def shards(
    adapter_input,
    output_gradient,
    projection,
    input_block_index,
    turn_token_length,
    turn_to_example,
):
    adapter_rows = adapter_input[0]
    grad_rows = output_gradient[0]
    proj_blocks = projection[0]
    picked = input_block_index[0]
    adapter_rank = adapter_rows.shape[0]
    count_of_tokens = grad_rows.shape[0]
    key_value_width = grad_rows.shape[1]
    shard_count = lax.axis_size("example")
    shard_owned_rows = EX_DEV // lax.axis_size("layer")
    owners = turn_to_example - lax.axis_index("example") * EX_DEV
    turn_ends = jnp.cumsum(turn_token_length)
    starts = turn_ends - turn_token_length
    position = jnp.arange(count_of_tokens, dtype=jnp.int32)
    inside = (
        (position[None, :] >= starts[:, None]) & (position[None, :] < turn_ends[:, None])
    ).astype(jnp.bfloat16)
    member = (owners[None, :] == jnp.arange(EX_DEV, dtype=jnp.int32)[:, None]).astype(jnp.bfloat16)
    ownership_mask = jnp.dot(member, inside, preferred_element_type=jnp.float32).astype(
        jnp.bfloat16
    )
    weighted_rows = (ownership_mask[:, None, :] * adapter_rows[None, :, :]).reshape(
        shard_owned_rows * lax.axis_size("layer") * adapter_rank, count_of_tokens
    )
    summed_total = jnp.dot(weighted_rows, grad_rows, preferred_element_type=jnp.float32)
    gradient_value = summed_total.reshape(
        shard_owned_rows * lax.axis_size("layer"), adapter_rank * key_value_width
    ).astype(jnp.bfloat16)
    pieces = []
    for column in range(proj_blocks.shape[0]):
        chosen = jnp.concatenate(
            [
                lax.dynamic_slice_in_dim(gradient_value, picked[column, slot_index] * 128, 128, 1)
                for slot_index in range(picked.shape[1])
            ],
            axis=1,
        )
        pieces.append(jnp.dot(chosen, proj_blocks[column], preferred_element_type=jnp.float32))
    features = lax.psum_scatter(
        jnp.concatenate(pieces, axis=1), "layer", scatter_dimension=0, tiled=True
    )
    local_gram = jnp.dot(
        features.T, features, precision=lax.Precision.HIGHEST, preferred_element_type=jnp.float32
    )
    gram_matrix = lax.psum(local_gram, ("layer", "example"))
    lower_factor = jnp.linalg.cholesky(gram_matrix)
    scale = math.sqrt(EX_DEV * shard_count)
    side_rows = gram_matrix.shape[0] // shard_count
    band = (
        lax.dynamic_slice_in_dim(
            lower_factor.T, lax.axis_index("example") * side_rows, side_rows, 0
        )
        / scale
    )
    whitened = jax.scipy.linalg.solve_triangular(lower_factor, features.T, lower=True).T * scale
    return (band, whitened)


def solution(mesh):
    in_specs = (
        P("layer", None, "example"),
        P("layer", "example", None),
        P("layer", None, None, None),
        P("layer", None, None),
        P("example"),
        P("example"),
    )
    out_specs = (P("example", None), P(("example", "layer"), None))
    return jax.shard_map(shards, mesh=mesh, in_specs=in_specs, out_specs=out_specs, check_vma=False)
```

profile of v0, /device:TPU:0, one launch (start us, length us, event | category | flops | bytes accessed | tf_op | source)
XLA Modules:
  0.0 321.7 jit_solution(10433597219825562685)
XLA Ops:
  7.2 2.0 fusion.93
  19.3 0.8 copy.15
  20.0 0.2 reduce-window.8
  20.3 0.7 sub.11
  21.0 0.7 broadcast_subtract_fusion
  21.6 0.7 convolution_convert_fusion
  22.4 4.6 %fusion.8 = bf16[512,512]{1,0:T(8,128)(2,1)S(1)} fusion(bf16[1,4096,512]{2,1,0:T(8,128)(2,1)} %param.7, bf16[8,4096]{1,0:T(8,128)(2,1)} %bitcast.100, bf16[64,4096]{1,0:T(8,128)(2,1)S(1)} %convolution_convert_fusion), kind=kOutput, calls=%fused_computation.12 | convolution fusion | flops 2149842944 | bytes 5308416 | tf_op jit(solution)/shard_map/dot_general | solution.py:42
  27.0 0.2 convert_element_type.13
  28.1 0.7 pad_maximum_fusion
  28.8 0.2 all-reduce.3.cloned.1.call-start
  29.1 12.9 %reduce-scatter.2.cloned.1.call-done = f32[32,512]{1,0:T(8,128)} async-done(((f32[64,512]{1,0:T(8,128)}), f32[32,512]{1,0:T(8,128)}) %reduce-scatter.2.cloned.1.call-update) | async-done | bytes 65552 | tf_op jit(solution)/shard_map/reduce_scatter | solution.py:56
  41.9 3.0 fusion.94
  45.0 132.1 %all-reduce.3.cloned.1.call-done = f32[512,512]{0,1:T(8,128)} async-done(((f32[512,512]{0,1:T(8,128)}), f32[512,512]{0,1:T(8,128)}) %all-reduce.3.cloned.1.call-update) | async-done | bytes 1048592 | tf_op jit(solution)/shard_map/psum | solution.py:62
  177.0 1.6 copy.17
  178.6 1.4 fusion.13
  180.1 11.7 %cholesky.104 = f32[128,128]{1,0:T(8,128)S(1)} custom-call(f32[128,128]{1,0:T(8,128)S(1)} %cholesky.266), custom_call_target="Cholesky" | custom-call | tf_op jit(solution)/shard_map/jit(cholesky)/cholesky | solution.py:63
  191.8 9.8 %custom-call.31 = f32[1,128,128]{1,2,0:T(8,128)S(1)} custom-call(f32[1,128,128]{2,1,0:T(8,128)S(1)} %get-tuple-element.51), custom_call_target="InvertDiagBlocksLowerTriangular" | custom-call | tf_op jit(solution)/shard_map/jit(cholesky)/cholesky | solution.py:63
  201.6 0.4 fusion.20
  202.2 0.5 convolution_subtract_fusion
  202.8 11.7 %cholesky.217 = f32[128,128]{1,0:T(8,128)S(1)} custom-call(f32[128,128]{1,0:T(8,128)S(1)} %cholesky.270), custom_call_target="Cholesky" | custom-call | tf_op jit(solution)/shard_map/jit(cholesky)/cholesky | solution.py:63
  214.6 9.8 %custom-call.32 = f32[1,128,128]{1,2,0:T(8,128)S(1)} custom-call(f32[1,128,128]{2,1,0:T(8,128)S(1)} %get-tuple-element.48), custom_call_target="InvertDiagBlocksLowerTriangular" | custom-call | tf_op jit(solution)/shard_map/jit(cholesky)/cholesky | solution.py:63
  224.4 0.3 convolution_dynamic-update-slice_fusion
  224.7 0.4 convolution_subtract_fusion.1
  225.1 11.7 %cholesky.238 = f32[128,128]{1,0:T(8,128)S(1)} custom-call(f32[128,128]{1,0:T(8,128)S(1)} %cholesky.275), custom_call_target="Cholesky" | custom-call | tf_op jit(solution)/shard_map/jit(cholesky)/cholesky | solution.py:63
  236.8 0.7 compare_reduce_fusion.1
  237.6 9.8 %custom-call.33 = f32[1,128,128]{1,2,0:T(8,128)S(1)} custom-call(f32[1,128,128]{2,1,0:T(8,128)S(1)} %get-tuple-element.45), custom_call_target="InvertDiagBlocksLowerTriangular" | custom-call | tf_op jit(solution)/shard_map/jit(cholesky)/cholesky | solution.py:63
  247.4 0.2 convolution_dynamic-update-slice_fusion.1
  247.6 0.4 convolution_subtract_fusion.2
  248.0 11.9 %cholesky.255 = f32[128,128]{1,0:T(8,128)S(1)} custom-call(f32[128,128]{1,0:T(8,128)S(1)} %convolution_subtract_fusion.2), custom_call_target="Cholesky" | custom-call | tf_op jit(solution)/shard_map/jit(cholesky)/cholesky | solution.py:63
  259.9 0.6 compare_reduce_fusion
  260.6 0.7 compare_reduce_fusion.2
  263.8 0.3 fusion.16
  264.1 8.5 %while.1 = (s32[]{:T(128)}, f32[512,512]{1,0:T(8,128)S(1)}, s32[4,2]{0,1:T(2,128)S(1)}, f32[4,128,128]{2,1,0:T(8,128)S(1)}, s32[]{:T(128)}) while((s32[]{:T(128)}, f32[512,512]{1,0:T(8,128)S(1)}, s32[4,2]{0,1:T(2,128)S(1)}, f32[4,128,128]{2,1,0:T(8,128)S(1)}, s32[]{:T(128)}) %tuple.63), condition=%wide.while_cond, body=%wide.while_body.sunk | while | flops 2 | bytes 131181 | solution.py:72
  264.1 0.6 fusion.103
  264.7 1.4 bitcast_dynamic-update-slice_fusion.2
  266.3 0.6 fusion.103
  266.9 1.4 bitcast_dynamic-update-slice_fusion.2
  268.4 0.6 fusion.103
  269.0 1.4 bitcast_dynamic-update-slice_fusion.2
  270.5 0.6 fusion.103
  271.1 1.4 bitcast_dynamic-update-slice_fusion.2
  272.5 39.3 %custom-call.34 = f32[4,128,128]{1,2,0:T(8,128)S(1)} custom-call(f32[4,128,128]{2,1,0:T(8,128)S(1)} %get-tuple-element.9), custom_call_target="InvertDiagBlocksLowerTriangular" | custom-call | tf_op jit(solution)/shard_map/jit(_solve_triangular)/triangular_solve | solution.py:72
  312.0 0.2 convolution_subtract_fusion.5
  312.4 0.2 convolution_subtract_fusion.4
  312.9 0.3 convolution_subtract_fusion.3
  313.2 0.2 fusion.37
  313.4 0.6 fusion.72
  314.2 0.7 copy.21
  (34 shorter events, 2.3 us)
Async XLA Ops:
  7.2 34.8 %reduce-scatter.2.cloned.1.call-start = ((), (), s32[]{:S(2)}) async-start(), calls=%async_computation.1 | async-start | bytes 196608 | tf_op jit(solution)/shard_map/reduce_scatter | solution.py:56
  22.4 5.1 %copy-start.1 = (bf16[1,4,512,128]{3,2,1,0:T(8,128)(2,1)S(1)}, bf16[1,4,512,128]{3,2,1,0:T(8,128)(2,1)}, u32[]{:S(2)}) copy-start(bf16[1,4,512,128]{3,2,1,0:T(8,128)(2,1)} %param.8) | copy-start | bytes 1572868
  28.8 148.2 %all-reduce.3.cloned.1.call-start = ((), (), s32[]{:S(2)}) async-start(), calls=%async_computation.2 | async-start | bytes 2097152 | tf_op jit(solution)/shard_map/psum | solution.py:62
  202.2 109.7 %copy-start = (f32[32,512]{1,0:T(8,128)S(1)}, f32[32,512]{1,0:T(8,128)}, u32[]{:S(2)}) copy-start(f32[32,512]{1,0:T(8,128)} %reduce-scatter.2.cloned.1.call-done) | copy-start | bytes 196612
Sparse Core Ops, SparseCore 0:
  28.9 12.9 reduce-scatter.1
  47.1 129.8 all-reduce.2
where the time goes:
time: 322 us
  waiting for transfers between devices  145 us (45%)
  other arithmetic  123 us (38%)
  between operations  27.1 us (8%)
  local copies, waits for them, and re-layouts  14.1 us (4%)
  matrix products  12.5 us (4%)
    psum x1, waiting for transfers between devices, shards(): gram_matrix = lax.psum(local_gram, ('layer', 'example'))  132 us
    another operation x14, other arithmetic, shards(): lower_factor = jnp.linalg.cholesky(gram_matrix)  78.6 us
    another operation x3, other arithmetic, shards(): jax.scipy.linalg.solve_triangular(lower_factor, features.T, lower=True)  39.6 us
    reduce_scatter x1, waiting for transfers between devices, shards(): lax.psum_scatter(jnp.concatenate(pieces, axis=1), 'layer', scatter_dimens...  12.9 us
    another operation x13, local copies, waits for them, and re-layouts  9.16 us
  transfers between devices with their start and end apart: 2, of which 2 were waited for; matrix products, arithmetic and copies ran while one was open for 0% of the time, Pallas kernels for 0%

commit v1 on v0

v1 whole, which is shorter than its diff:
```python
import functools
import math

import jax
import jax.numpy as jnp
from jax import lax
from jax.experimental import pallas as pl
from jax.experimental.pallas import tpu as pltpu
from jax.sharding import PartitionSpec as P

EX_DEV = 64
LANES = 128
F32 = jnp.float32
BF16 = jnp.bfloat16
MESH = pl.DeviceIdType.MESH


def mm(a, b):
    return jnp.dot(a, b, preferred_element_type=F32)


def mm_t(a, b):
    return lax.dot_general(a, b, (((1,), (1,)), ((), ())), preferred_element_type=F32)


def mm_tn(a, b):
    return lax.dot_general(a, b, (((0,), (0,)), ((), ())), preferred_element_type=F32)


def split(x):
    high = x.astype(BF16)
    return high, (x - high.astype(F32)).astype(BF16)


def three(dot, a, b):
    return dot(a[0], b[0]) + (dot(a[0], b[1]) + dot(a[1], b[0]))


def gram_kernel(
    layers, shards, pieces, chunk,
    idx_ref, lens_ref, own_ref, a_ref, g_hbm, proj_ref,
    gram_ref, feat_ref,
    g_buf, acc, grad, part, part_in, both, packed, rs_in,
    g_sem, px_send, px_recv, fx_send, fx_recv, rs_send, rs_recv,
    ag_send, ag_recv, xf_send, xf_recv, cf_send, cf_recv,
):
    layer = lax.axis_index("layer")
    shard = lax.axis_index("example")
    peers = shards // 2
    spot = shard // 2
    core = shard % 2
    mate = spot * 2 + (1 - core)

    def to_layer(d):
        return ((layer + d) % layers, shard)

    def to_spot(d):
        return (layer, ((spot + d) % peers) * 2 + core)

    loads = []
    rows = g_hbm.shape[0] // pieces
    for i in range(pieces):
        cut = pl.ds(i * rows, rows)
        load = pltpu.make_async_copy(g_hbm.at[cut], g_buf.at[cut], g_sem.at[i])
        load.start()
        loads.append(load)

    barrier = pltpu.get_barrier_semaphore()
    targets = [to_layer(d) for d in range(1, layers)]
    targets += [to_spot(d) for d in range(1, peers)] + [(layer, mate)]
    for target in targets:
        pl.semaphore_signal(barrier, inc=1, device_id=target, device_id_type=MESH)

    lens = lens_ref[...].astype(F32)
    local = own_ref[...] - shard * EX_DEV
    example = lax.broadcasted_iota(jnp.int32, (EX_DEV, lens.shape[1]), 0)
    start = jnp.sum(jnp.where(local < example, lens, 0.0), axis=1, keepdims=True)
    end = jnp.sum(jnp.where(local <= example, lens, 0.0), axis=1, keepdims=True)
    rank = a_ref.shape[0]
    for i in range(pieces):
        place = (lax.broadcasted_iota(jnp.int32, (EX_DEV, rows), 1) + i * rows).astype(F32)
        mask = jnp.where((place >= start) & (place < end), 1.0, 0.0).astype(BF16)
        weighted = jnp.concatenate(
            [mask * a_ref[r : r + 1, i * rows : (i + 1) * rows] for r in range(rank)], axis=0
        )
        loads[i].wait()
        product = mm(weighted, g_buf[i * rows : (i + 1) * rows, :])
        if i == 0:
            acc[...] = product
        else:
            acc[...] += product
    width = g_hbm.shape[1] // LANES
    for r in range(rank):
        for w in range(width):
            grad[r * width + w] = acc[
                r * EX_DEV : (r + 1) * EX_DEV, w * LANES : (w + 1) * LANES
            ].astype(BF16)
    blocks, depth = proj_ref.shape[0], proj_ref.shape[1] // LANES
    for j in range(blocks):
        chosen = jnp.concatenate([grad[idx_ref[j, k]] for k in range(depth)], axis=1)
        part[:, j * LANES : (j + 1) * LANES] = mm(chosen, proj_ref[j])

    pl.semaphore_wait(barrier, len(targets))
    sends = []

    def push(src, dst, send_sem, recv_sem, target):
        copy = pltpu.make_async_remote_copy(
            src_ref=src, dst_ref=dst, send_sem=send_sem, recv_sem=recv_sem,
            device_id=target, device_id_type=MESH,
        )
        copy.start()
        sends.append(copy)
        return copy

    copies = [
        push(part, part_in.at[d - 1], px_send.at[d - 1], px_recv.at[d - 1], to_layer(d))
        for d in range(1, layers)
    ]
    for copy in copies:
        copy.wait_recv()
    total = part[...]
    for d in range(1, layers):
        total = total + part_in[d - 1]
    both[0] = total

    copy = push(both.at[0], both.at[1], fx_send, fx_recv, (layer, mate))
    owned = EX_DEV // layers
    feat_ref[...] = both[0, pl.ds(pl.multiple_of(layer * owned, 8), owned), :]
    copy.wait_recv()

    pair = jnp.concatenate([both[0], both[1]], axis=0)
    high, low = split(pair)
    row = 0
    for i in range(blocks):
        cut = slice(i * LANES, (i + 1) * LANES)
        strip = three(
            mm_tn, (high[:, cut], low[:, cut]), (high[:, i * LANES :], low[:, i * LANES :])
        )
        for j in range(blocks - i):
            packed[row : row + LANES, :] = strip[:, j * LANES : (j + 1) * LANES]
            row += LANES
    if row < packed.shape[0]:
        packed[row:, :] = jnp.zeros((packed.shape[0] - row, LANES), F32)

    def where(lay, cor, spo):
        return pl.multiple_of(((lay * 2 + cor) * peers + spo) * chunk, 8)

    mine = where(layer, core, spot)
    copies = []
    for d in range(1, peers):
        source = where(layer, core, (spot + d) % peers)
        copies.append(push(
            packed.at[pl.ds(source, chunk)], rs_in.at[d - 1],
            rs_send.at[d - 1], rs_recv.at[d - 1], to_spot(d),
        ))
    total = packed[pl.ds(mine, chunk), :]
    for d in range(1, peers):
        copies[d - 1].wait_recv()
        total = total + rs_in[d - 1]
    gram_ref[pl.ds(mine, chunk), :] = total

    gathers = []
    here = gram_ref.at[pl.ds(mine, chunk)]
    for d in range(1, peers):
        gathers.append(push(here, here, ag_send.at[d - 1], ag_recv.at[d - 1], to_spot(d)))
    forwards = []
    for d in range(peers):
        if d:
            gathers[d - 1].wait_recv()
        got = gram_ref.at[pl.ds(where(layer, core, (spot - d + peers) % peers), chunk)]
        for x in range(1, layers):
            forwards.append(push(got, got, xf_send.at[x - 1, d], xf_recv.at[x - 1, d], to_layer(x)))
    pairs = []
    for x in range(layers):
        if x:
            for d in range(peers):
                forwards[d * (layers - 1) + x - 1].wait_recv()
        got = gram_ref.at[pl.ds(where((layer - x + layers) % layers, core, 0), peers * chunk)]
        pairs.append(push(got, got, cf_send.at[x], cf_recv.at[x], (layer, mate)))
    for copy in pairs:
        copy.wait_recv()
    for copy in sends:
        copy.wait_send()


def diagonal(shape):
    return lax.broadcasted_iota(jnp.int32, shape, 0) == lax.broadcasted_iota(jnp.int32, shape, 1)


def factor_kernel(
    scale, blocks, gram_ref, feat_ref, band_ref, white_ref,
    full, b_high, b_low, x_ref, inv, work,
):
    size = blocks * LANES
    half = size // 2
    row = 0
    for i in range(blocks):
        for j in range(i, blocks):
            block = gram_ref[row : row + LANES, :]
            row += LANES
            full[i * LANES : (i + 1) * LANES, j * LANES : (j + 1) * LANES] = block
            if j > i:
                full[j * LANES : (j + 1) * LANES, i * LANES : (i + 1) * LANES] = block.T
    gram = full[...]
    eye = diagonal((size, size))
    kept = jnp.where(eye, gram, 0.0)
    inv_row = lax.rsqrt(jnp.sum(kept, axis=0, keepdims=True))
    inv_col = lax.rsqrt(jnp.sum(kept, axis=1, keepdims=True))
    inv[...] = inv_row
    scaled = gram * inv_col * inv_row
    full[...] = scaled
    high, low = split(scaled)
    b_high[...] = high
    b_low[...] = low
    bound = jnp.max(jnp.sum(jnp.abs(scaled), axis=0, keepdims=True))
    first = 2.5 / jnp.full((1, size), bound, F32)
    rows = lax.broadcasted_iota(jnp.int32, (size, size), 0)
    cols = lax.broadcasted_iota(jnp.int32, (size, size), 1)
    root = jnp.sqrt(first)
    x_ref[...] = jnp.where(
        rows > cols, -first * scaled * root,
        jnp.where(eye, root * (1.5 - 0.5 * first * scaled), 0.0),
    )

    corner = diagonal((half, half))
    lower = lax.broadcasted_iota(jnp.int32, (half, half), 0) > lax.broadcasted_iota(
        jnp.int32, (half, half), 1
    )
    ident = jnp.where(corner, 1.0, 0.0)

    def half_low(e):
        return jnp.where(lower, e, jnp.where(corner, 0.5 * e, 0.0))

    def step(fine):
        top = x_ref[:half, :half]
        bottom = x_ref[half:, :]
        bh = b_high[...]
        if fine:
            bl = b_low[...]
            top_s, bottom_s = split(top), split(bottom)
            y0 = three(mm, top_s, (bh[:half, :half], bl[:half, :half]))
            y1 = three(mm, bottom_s, (bh, bl))
            y0_s, y1_s = split(y0), split(y1)
            e0 = three(mm_t, y0_s, top_s) - ident
            e1 = three(mm_t, (y1_s[0][:, :half], y1_s[1][:, :half]), top_s)
            e2 = three(mm_t, y1_s, bottom_s) - ident
            top_h, bottom_h = top_s[0], bottom_s[0]
        else:
            top_h, bottom_h = top.astype(BF16), bottom.astype(BF16)
            y0 = mm(top_h, bh[:half, :half]).astype(BF16)
            y1 = mm(bottom_h, bh).astype(BF16)
            e0 = mm_t(y0, top_h) - ident
            e1 = mm_t(y1[:, :half], top_h)
            e2 = mm_t(y1, bottom_h) - ident
        p0 = half_low(e0).astype(BF16)
        p1 = e1.astype(BF16)
        p2 = half_low(e2).astype(BF16)
        x_ref[:half, :half] = top - mm(p0, top_h)
        x_ref[half:, :half] = bottom[:, :half] - (mm(p1, top_h) + mm(p2, bottom_h[:, :half]))
        x_ref[half:, half:] = bottom[:, half:] - mm(p2, bottom_h[:, half:])
        return e0, e1, e2

    def norm(errors):
        e0, e1, e2 = errors
        return jnp.sum(e0 * e0 + 2.0 * (e1 * e1) + e2 * e2)

    def body(fine, state):
        return state[0] + 1, norm(step(fine))

    def blind(_, carry):
        step(False)
        return carry

    lax.fori_loop(0, 6, blind, 0)
    state = lax.while_loop(
        lambda s: (s[0] < 24) & jnp.logical_not(s[1] < 1.0),
        functools.partial(body, False), (jnp.int32(0), F32(1e9)),
    )
    state = lax.while_loop(
        lambda s: (s[0] < 8) & jnp.logical_not(s[1] < 1e-4),
        functools.partial(body, True), (jnp.int32(0), F32(1e9)),
    )
    good = state[1] < 1e-4

    @pl.when(jnp.logical_not(good))
    def _():
        work[:, :size] = full[...]
        work[:, size:] = jnp.where(eye, 1.0, 0.0)
        line = lax.broadcasted_iota(jnp.int32, (1, 2 * size), 1)
        down = lax.broadcasted_iota(jnp.int32, (size, 1), 0)

        def column(j, carry):
            pivot_row = work[pl.ds(j, 1), :]
            pivot = jnp.sum(jnp.where(line == j, pivot_row, 0.0), axis=1, keepdims=True)
            pivot_row = pivot_row / jnp.sqrt(pivot)
            left = work[:, :size]
            entry = jnp.sum(jnp.where(cols == j, left, 0.0), axis=1, keepdims=True)
            entry = jnp.where(down > j, entry / jnp.sqrt(pivot), 0.0)
            work[...] = work[...] - entry * pivot_row
            work[pl.ds(j, 1), :] = pivot_row
            return carry

        lax.fori_loop(0, size, column, 0)
        x_ref[...] = jnp.where(rows >= cols, work[:, size:], 0.0)

    side = band_ref.shape[0]
    begin = pl.multiple_of(lax.axis_index("example") * side, 8)
    over = 1.0 / (inv[...] * scale)
    band_rows = lax.broadcasted_iota(jnp.int32, (side, size), 0) + begin
    upper = lax.broadcasted_iota(jnp.int32, (side, size), 1) >= band_rows

    @pl.when(good)
    def _():
        band = three(mm, split(x_ref[pl.ds(begin, side), :]), (b_high[...], b_low[...]))
        band_ref[...] = jnp.where(upper, band * over, 0.0)

    @pl.when(jnp.logical_not(good))
    def _():
        band_ref[...] = jnp.where(upper, work[pl.ds(begin, side), :size] * over, 0.0)

    white_ref[...] = scale * three(mm_t, split(feat_ref[...] * inv[...]), split(x_ref[...]))


def shards(
    adapter_input,
    output_gradient,
    projection,
    input_block_index,
    turn_token_length,
    turn_to_example,
):
    layers, count = lax.axis_size("layer"), lax.axis_size("example")
    rank, tokens = adapter_input.shape[1:]
    width = output_gradient.shape[2]
    blocks, depth, _ = projection.shape[1:]
    size = blocks * LANES
    peers = count // 2
    pieces = 4
    packed_rows = blocks * (blocks + 1) // 2 * LANES
    owners = 2 * layers * peers
    chunk = -(-packed_rows // (owners * 8)) * 8
    vmem = pl.BlockSpec(memory_space=pltpu.VMEM)
    dma = pltpu.SemaphoreType.DMA
    near, far = max(layers - 1, 1), max(peers - 1, 1)
    gram, features = pl.pallas_call(
        functools.partial(gram_kernel, layers, count, pieces, chunk),
        out_shape=(
            jax.ShapeDtypeStruct((owners * chunk, LANES), F32),
            jax.ShapeDtypeStruct((EX_DEV // layers, size), F32),
        ),
        in_specs=[
            pl.BlockSpec(memory_space=pltpu.SMEM), vmem, vmem, vmem,
            pl.BlockSpec(memory_space=pl.ANY), vmem,
        ],
        out_specs=(vmem, vmem),
        scratch_shapes=[
            pltpu.VMEM((tokens, width), BF16),
            pltpu.VMEM((rank * EX_DEV, width), F32),
            pltpu.VMEM((rank * width // LANES, EX_DEV, LANES), BF16),
            pltpu.VMEM((EX_DEV, size), F32),
            pltpu.VMEM((near, EX_DEV, size), F32),
            pltpu.VMEM((2, EX_DEV, size), F32),
            pltpu.VMEM((owners * chunk, LANES), F32),
            pltpu.VMEM((far, chunk, LANES), F32),
            dma((pieces,)),
            dma((near,)), dma((near,)), dma(()), dma(()),
            dma((far,)), dma((far,)), dma((far,)), dma((far,)),
            dma((near, peers)), dma((near, peers)), dma((layers,)), dma((layers,)),
        ],
        compiler_params=pltpu.CompilerParams(
            collective_id=0, has_side_effects=True, vmem_limit_bytes=40 * 1024 * 1024
        ),
    )(
        input_block_index[0],
        turn_token_length.reshape(1, -1),
        turn_to_example.reshape(1, -1),
        adapter_input[0],
        output_gradient[0],
        projection[0],
    )
    return pl.pallas_call(
        functools.partial(factor_kernel, math.sqrt(EX_DEV * count), blocks),
        out_shape=(
            jax.ShapeDtypeStruct((size // count, size), F32),
            jax.ShapeDtypeStruct((EX_DEV // layers, size), F32),
        ),
        in_specs=[vmem, vmem],
        out_specs=(vmem, vmem),
        scratch_shapes=[
            pltpu.VMEM((size, size), F32),
            pltpu.VMEM((size, size), BF16),
            pltpu.VMEM((size, size), BF16),
            pltpu.VMEM((size, size), F32),
            pltpu.VMEM((1, size), F32),
            pltpu.VMEM((size, 2 * size), F32),
        ],
        compiler_params=pltpu.CompilerParams(vmem_limit_bytes=40 * 1024 * 1024),
    )(gram, features)


def solution(mesh):
    in_specs = (
        P("layer", None, "example"),
        P("layer", "example", None),
        P("layer", None, None, None),
        P("layer", None, None),
        P("example"),
        P("example"),
    )
    out_specs = (P("example", None), P(("example", "layer"), None))
    return jax.shard_map(shards, mesh=mesh, in_specs=in_specs, out_specs=out_specs, check_vma=False)
```

time: 322 us -> 46.9 us (0.15)
  waiting for transfers between devices: 145 us -> 0 us
  other arithmetic: 123 us -> 0 us
  Pallas kernels: 0 us -> 39.9 us
  between operations: 27.1 us -> 0.65 us
  matrix products: 12.5 us -> 0 us
  local copies, waits for them, and re-layouts: 14.1 us -> 6.05 us
    psum x1 -> x0, waiting for transfers between devices: 132 us -> none  [shards(): gram_matrix = lax.psum(local_gram, ('layer', 'example'))]
    another operation x19 -> x0, other arithmetic: 119 us -> none  [the longest x14 78.6 us: shards(): lower_factor = jnp.linalg.cholesky(gram_matrix)]
    pallas_call x0 -> x2, Pallas kernels: none -> 39.9 us  [the longest x1 27.9 us: shards(): pl.pallas_call(functools.partial(gram_kernel, layers, count, pieces, chun...]
    reduce_scatter x1 -> x0, waiting for transfers between devices: 12.9 us -> none  [shards(): lax.psum_scatter(jnp.concatenate(pieces, axis=1), 'layer', scatter_dimens...]
    another operation x20 -> x0, local copies, waits for them, and re-layouts: 9.44 us -> none
    dot_general x7 -> x0, matrix products: 8.96 us -> none  [the longest x1 4.61 us: shards(): jnp.dot(weighted_rows, grad_rows, preferred_element_type=jnp.float32)]
    unnamed x5 -> x12, local copies, waits for them, and re-layouts: 0.75 us -> 6.05 us
    another operation x13 -> x0, matrix products: 3.57 us -> none  [the longest x6 2.13 us: shards(): lower_factor = jnp.linalg.cholesky(gram_matrix)]
  transfers between devices with their start and end apart: 2 -> 0, of which waited for: 2 -> 0; matrix products, arithmetic and copies ran while one was open for 0% -> 0% of each run, Pallas kernels for 0% -> 0%
where the time goes in v1:
time: 46.9 us; the launch traced here: 46.6 us
  Pallas kernels  39.9 us (85%)
  local copies, waits for them, and re-layouts  6.05 us (13%)
  between operations  0.65 us (1%)
    pallas_call x1, Pallas kernels, shards(): pl.pallas_call(functools.partial(gram_kernel, layers, count, pieces, chun...  27.9 us
    pallas_call x1, Pallas kernels, shards(): pl.pallas_call(functools.partial(factor_kernel, math.sqrt(EX_DEV * count)...  12 us
    unnamed x12, local copies, waits for them, and re-layouts  6.05 us

profile of v1, /device:TPU:0, one launch (start us, length us, event | category | flops | bytes accessed | tf_op | source)
XLA Modules:
  0.0 46.6 jit_solution(1377264478460622675)
XLA Ops:
  0.6 0.0 copy-start
  0.6 2.2 %copy-done = bf16[1,4096,512]{2,1,0:T(8,128)(2,1)S(1)} copy-done((bf16[1,4096,512]{2,1,0:T(8,128)(2,1)S(1)}, bf16[1,4096,512]{2,1,0:T(8,128)(2,1)}, u32[]{:S(2)}) %copy-start) | copy-done | bytes 4194328
  2.8 0.0 copy-start.1
  2.8 1.0 %copy-done.1 = bf16[1,4,512,128]{3,2,1,0:T(8,128)(2,1)S(1)} copy-done((bf16[1,4,512,128]{3,2,1,0:T(8,128)(2,1)S(1)}, bf16[1,4,512,128]{3,2,1,0:T(8,128)(2,1)}, u32[]{:S(2)}) %copy-start.1) | copy-done | bytes 524312
  3.9 0.0 copy-start.2
  3.9 0.8 %copy-done.2 = bf16[1,8,4096]{2,1,0:T(8,128)(2,1)S(1)} copy-done((bf16[1,8,4096]{2,1,0:T(8,128)(2,1)S(1)}, bf16[1,8,4096]{2,1,0:T(8,128)(2,1)}, u32[]{:S(2)}) %copy-start.2) | copy-done | bytes 65560
  4.7 0.0 copy-start.3
  4.7 0.7 %copy-done.3 = s32[1,4,4]{2,1,0:T(4,128)S(1)} copy-done((s32[1,4,4]{2,1,0:T(4,128)S(1)}, s32[1,4,4]{2,1,0:T(4,128)}, u32[]{:S(2)}) %copy-start.3) | copy-done | bytes 88
  5.4 0.0 copy-start.4
  5.4 0.7 %copy-done.4 = s32[128]{0:T(128)S(1)} copy-done((s32[128]{0:T(128)S(1)}, s32[128]{0:T(128)}, u32[]{:S(2)}) %copy-start.4) | copy-done | bytes 536
  6.0 0.0 copy-start.5
  6.0 0.7 %copy-done.5 = s32[128]{0:T(128)S(1)} copy-done((s32[128]{0:T(128)S(1)}, s32[128]{0:T(128)}, u32[]{:S(2)}) %copy-start.5) | copy-done | bytes 536
  6.7 27.9 %shard_map.77 = (f32[1280,128]{1,0:T(8,128)S(1)}, f32[32,512]{1,0:T(8,128)S(1)}) custom-call(s32[4,4]{1,0:T(4,128)S(1)} %bitcast.9, s32[1,128]{1,0:T(1,128)S(1)} %bitcast.10, s32[1,128]{1,0:T(1,128)S(1)} %bitcast.11, bf16[8,4096]{1,0:T(8,128)(2,1)S(1)} %bitcast.8, bf16[4096,512]{1,0:T(8,128)(2,1)S(1)} %bitcast.6, bf16[4,512,128]{2,1,0:T(8,128)(2,1)S(1)} %bitcast.7), custom_call_target="tpu_custom_call" | custom-call | tf_op jit(solution)/shard_map/pallas_call | solution.py:345
  34.6 12.0 %shard_map.78 = (f32[32,512]{1,0:T(8,128)}, f32[32,512]{1,0:T(8,128)}) custom-call(f32[1280,128]{1,0:T(8,128)S(1)} %get-tuple-element.4.gram_ref, f32[32,512]{1,0:T(8,128)S(1)} %get-tuple-element.5.feat_ref), custom_call_target="tpu_custom_call" | custom-call | tf_op jit(solution)/shard_map/pallas_call | solution.py:381
Async XLA Ops:
  0.6 2.2 %copy-start = (bf16[1,4096,512]{2,1,0:T(8,128)(2,1)S(1)}, bf16[1,4096,512]{2,1,0:T(8,128)(2,1)}, u32[]{:S(2)}) copy-start(bf16[1,4096,512]{2,1,0:T(8,128)(2,1)} %param.7) | copy-start | bytes 12582916
  2.8 1.0 %copy-start.1 = (bf16[1,4,512,128]{3,2,1,0:T(8,128)(2,1)S(1)}, bf16[1,4,512,128]{3,2,1,0:T(8,128)(2,1)}, u32[]{:S(2)}) copy-start(bf16[1,4,512,128]{3,2,1,0:T(8,128)(2,1)} %param.8) | copy-start | bytes 1572868
  3.9 0.8 %copy-start.2 = (bf16[1,8,4096]{2,1,0:T(8,128)(2,1)S(1)}, bf16[1,8,4096]{2,1,0:T(8,128)(2,1)}, u32[]{:S(2)}) copy-start(bf16[1,8,4096]{2,1,0:T(8,128)(2,1)} %param.6) | copy-start | bytes 196612
  4.7 0.7 %copy-start.3 = (s32[1,4,4]{2,1,0:T(4,128)S(1)}, s32[1,4,4]{2,1,0:T(4,128)}, u32[]{:S(2)}) copy-start(s32[1,4,4]{2,1,0:T(4,128)} %param.9) | copy-start | bytes 196
  5.4 0.7 %copy-start.4 = (s32[128]{0:T(128)S(1)}, s32[128]{0:T(128)}, u32[]{:S(2)}) copy-start(s32[128]{0:T(128)} %param.10) | copy-start | bytes 1540
  6.0 0.7 %copy-start.5 = (s32[128]{0:T(128)S(1)}, s32[128]{0:T(128)}, u32[]{:S(2)}) copy-start(s32[128]{0:T(128)} %param.11) | copy-start | bytes 1540
